TPU v7x, 32 devices: a whole 2x2x4 slice. The times are simulated.
32 devices in a mesh: die: 2 (over y), row: 4 (over z), col: 4 (over x, core).
Axes of the slice: x: 2, y: 2, z: 4, core: 2. Of those that a mesh axis runs over, the one named last changes fastest.
Arguments:
- parcel_patch: float32 [4, 2048, 256], P('die', ('row', 'col')), may hold values from 0.1 to 1
- target_unit: int32 [4, 2048, 1], P('die', ('row', 'col')), may hold values from 0 to 15; in each aligned block of 128 rows (0 to 127, 128 to 255, ..., all dimensions but the last counted through in order) at most 16 rows name the same one
- target_patch: int32 [4, 2048], P('die', ('row', 'col')), may hold values from 0 to 127
- across_taps: float32 [8, 255], replicated, may hold values from -0.375 to 0.375
- down_taps: float32 [8, 255], replicated, may hold values from -0.375 to 0.375
- source_heated_mixing: float32 [8, 4, 4], replicated, may hold values from -2.4 to 2.4
Outputs:
- chip_heat_increase: float32 [4, 512, 1024], P('die', 'row', 'col')
- block_power_slopes: float32 [4, 2048, 256], P('die', ('row', 'col'))
Inputs may be any that keep to these rules, and one draw needn't show every extreme that they name: `target_unit`: among the 128 blocks of one die held by one device (aligned blocks of rows), at most 16 name the same device, and in every draw some such group names one device exactly 16 times.
All inputs are finite; a program needn't handle non-finite values.
Results may differ from a plain program's by a relative error of at most 0.0002.
Values sent between devices are 32-bit elements; how exact they have to be, the bound alone decides.
A program may use at most 192 MiB of HBM per device.

v0:
```python
import functools

import jax
import jax.numpy as jnp
from jax import lax
from jax.experimental import pallas as pl
from jax.experimental.pallas import tpu as pltpu
from jax.sharding import PartitionSpec as P

PATCH_SIDE = 16
UNIT_MESH_X = 128
UNIT_MESH_Y = 256
HALO = 128


high = lax.Precision.HIGH


def two_halves(values):
    head = values.astype(jnp.bfloat16)
    return head, (values - head.astype(jnp.float32)).astype(jnp.bfloat16)


def stage_kernel(
    is_seed, x_ref, across_ref, down_ref, mix_ref, out_ref,
    pad, a_cat, d_cat, p_cat, y_all, acc, got, send, recv,
):
    here, a, b = x_ref.shape
    terms = across_ref.shape[0]
    h = HALO
    row, col, die = lax.axis_index("row"), lax.axis_index("col"), lax.axis_index("die")
    has_up, has_down = row > 0, row < lax.axis_size("row") - 1
    has_left, has_right = col > 0, col < lax.axis_size("col") - 1
    up, down, left, right = {"row": row - 1}, {"row": row + 1}, {"col": col - 1}, {"col": col + 1}
    other = {"die": 1 - die}
    near = ((has_up, up), (has_down, down), (has_left, left), (has_right, right))

    pad[...] = jnp.zeros_like(pad)
    own = x_ref[...]
    pad[:, h : h + a, h : h + b] = jax.nn.sigmoid(own) if is_seed else own

    barrier = pltpu.get_barrier_semaphore()
    for there, device in near:
        @pl.when(there)
        def _(device=device):
            pl.semaphore_signal(barrier, inc=1, device_id=device, device_id_type=pl.DeviceIdType.MESH)
    pl.semaphore_signal(barrier, inc=1, device_id=other, device_id_type=pl.DeviceIdType.MESH)
    count = jnp.int32(1)
    for there, _ in near:
        count = count + there.astype(jnp.int32)
    pl.semaphore_wait(barrier, count)

    def copy(number, src, dst, device):
        return pltpu.make_async_remote_copy(
            src_ref=src, dst_ref=dst, send_sem=send.at[number], recv_sem=recv.at[number],
            device_id=device, device_id_type=pl.DeviceIdType.MESH,
        )

    tops = (0, h, h + a)
    sizes = (h, a, h)

    def block(band, start, width):
        return pad.at[:, pl.ds(tops[band], sizes[band]), pl.ds(start, width)]

    to_up = copy(0, pad.at[:, pl.ds(h, h), pl.ds(h, b)], block(2, h, b), up)
    to_down = copy(1, pad.at[:, pl.ds(a, h), pl.ds(h, b)], block(0, h, b), down)
    to_left = [copy(2 + k, block(k, h, h), block(k, h + b, h), left) for k in range(3)]
    to_right = [copy(5 + k, block(k, b, h), block(k, 0, h), right) for k in range(3)]

    def start(there, c):
        @pl.when(there)
        def _():
            c.start()

    def ended(there, c):
        @pl.when(there)
        def _():
            c.wait_send()

    def arrived(there, c):
        @pl.when(there)
        def _():
            c.wait_recv()

    start(has_up, to_up)
    start(has_down, to_down)
    start(has_left, to_left[1])
    start(has_right, to_right[1])

    def across_bands(t):
        span = jnp.broadcast_to(across_ref[pl.ds(t, 1), :], (a, a + 2 * h))
        head, rest = two_halves(pltpu.roll(span, 0, 1, stride=1, stride_axis=0))
        lines = pl.ds(t * a, a)
        w = a + 2 * h
        a_cat[lines, 0:w] = head
        a_cat[lines, w : 2 * w] = head
        a_cat[lines, 2 * w : 3 * w] = rest

    def down_bands(t):
        w = b + 2 * h
        span = jnp.broadcast_to(down_ref[pl.ds(t, 1), :], (h, 3 * h))
        head, rest = two_halves(pltpu.roll(span, 0, 1, stride=1, stride_axis=0))
        for part in range(3):
            piece = rest if part == 1 else head
            for k in range(b // h):
                lo, hi = k * h, k * h + 3 * h
                lines = pl.ds(k * h, h)
                d_cat[t, lines, part * w + lo : part * w + hi] = piece
                if lo:
                    d_cat[t, lines, part * w : part * w + lo] = jnp.zeros((h, lo), jnp.bfloat16)
                if hi < w:
                    d_cat[t, lines, part * w + hi : part * w + w] = jnp.zeros((h, w - hi), jnp.bfloat16)

    for t in range(terms):
        across_bands(t)
    arrived(has_down, to_up)
    for c, there in ((to_left[2], has_left), (to_right[2], has_right)):
        start(jnp.logical_and(has_down, there), c)
    arrived(has_up, to_down)
    for c, there in ((to_left[0], has_left), (to_right[0], has_right)):
        start(jnp.logical_and(has_up, there), c)
    for t in range(terms):
        down_bands(t)
    rows_of = (has_up, None, has_down)
    for k in range(3):
        for there, c in ((has_right, to_left[k]), (has_left, to_right[k])):
            arrived(there if k == 1 else jnp.logical_and(rows_of[k], there), c)

    w0, w1 = a + 2 * h, b + 2 * h
    for e in range(here):
        head, rest = two_halves(pad[e])
        cols = pl.ds(e * w1, w1)
        p_cat[0:w0, cols] = head
        p_cat[w0 : 2 * w0, cols] = rest
        p_cat[2 * w0 : 3 * w0, cols] = head

    def across(n, carry):
        cols = pl.ds(pl.multiple_of(n * 256, 256), 256)
        y_all[:, cols] = jnp.dot(a_cat[...], p_cat[:, cols], preferred_element_type=jnp.float32)
        return carry

    lax.fori_loop(0, here * w1 // 256, across, 0)
    acc[...] = jnp.zeros_like(acc)

    def along(t, carry):
        lines = pl.ds(pl.multiple_of(t * a, a), a)
        rows = jnp.concatenate([y_all[lines, e * w1 : (e + 1) * w1] for e in range(here)], axis=0)
        head, rest = two_halves(rows)
        z = lax.dot_general(
            jnp.concatenate([head, head, rest], axis=1), d_cat[t],
            (((1,), (1,)), ((), ())), preferred_element_type=jnp.float32,
        )
        for d in range(acc.shape[0]):
            total = acc[d]
            for e in range(here):
                total = total + mix_ref[t, d * here + e] * z[e * a : (e + 1) * a]
            acc[d] = total
        return carry

    lax.fori_loop(0, terms, along, 0)
    share = copy(8, acc.at[pl.ds((1 - die) * here, here)], got, other)
    share.start()
    for there, c in ((has_up, to_up), (has_down, to_down), (has_left, to_left[1]), (has_right, to_right[1])):
        ended(there, c)
    for k in (0, 2):
        for there, c in ((has_left, to_left[k]), (has_right, to_right[k])):
            ended(jnp.logical_and(rows_of[k], there), c)
    share.wait()
    out_ref[...] = acc[pl.ds(die * here, here)] + got[...]


def bases(taps):
    return jnp.pad(taps, ((0, 0), (1, 3 * HALO - 1 - taps.shape[1])))


def stage(fields, across_taps, down_taps, mix, is_seed):
    here, a, b = fields.shape
    terms, dies, _ = mix.shape
    w0, w1 = a + 2 * HALO, b + 2 * HALO
    vmem = pl.BlockSpec(memory_space=pltpu.VMEM)
    return pl.pallas_call(
        functools.partial(stage_kernel, is_seed),
        out_shape=jax.ShapeDtypeStruct(fields.shape, jnp.float32),
        in_specs=[vmem, vmem, vmem, pl.BlockSpec(memory_space=pltpu.SMEM)],
        out_specs=vmem,
        scratch_shapes=[
            pltpu.VMEM((here, w0, w1), jnp.float32),
            pltpu.VMEM((terms * a, 3 * w0), jnp.bfloat16),
            pltpu.VMEM((terms, b, 3 * w1), jnp.bfloat16),
            pltpu.VMEM((3 * w0, here * w1), jnp.bfloat16),
            pltpu.VMEM((terms * a, here * w1), jnp.float32),
            pltpu.VMEM((dies, a, b), jnp.float32),
            pltpu.VMEM((here, a, b), jnp.float32),
            pltpu.SemaphoreType.DMA((9,)),
            pltpu.SemaphoreType.DMA((9,)),
        ],
        compiler_params=pltpu.CompilerParams(
            collective_id=1 if is_seed else 0, has_side_effects=True, vmem_limit_bytes=48 * 2**20
        ),
    )(fields, bases(across_taps), bases(down_taps), mix.reshape(terms, dies * here))


def tiles_to_map(patch_totals_acc, tiles_down):
    dies_here, tile_total, cell_count = patch_totals_acc.shape
    mesh_layout = patch_totals_acc.reshape(
        dies_here, tile_total // tiles_down, tiles_down, PATCH_SIDE, PATCH_SIDE
    )
    return mesh_layout.transpose(0, 1, 3, 2, 4).reshape(
        dies_here, tile_total // tiles_down * PATCH_SIDE, tiles_down * PATCH_SIDE
    )


def map_to_tiles(source, tiles_down):
    dies_here, rows_all, cols_all = source.shape
    mesh_layout = source.reshape(
        dies_here, rows_all // PATCH_SIDE, PATCH_SIDE, tiles_down, PATCH_SIDE
    )
    return mesh_layout.transpose(0, 1, 3, 2, 4).reshape(dies_here, -1, PATCH_SIDE * PATCH_SIDE)


def local(parcel_patch, target_unit, target_patch, across_taps, down_taps, source_heated_mixing):
    dies_here, blocks_here, cells_tile = parcel_patch.shape
    devices_grid = lax.axis_size(("row", "col"))
    capacity = max(2, 2 * blocks_here // devices_grid)
    tiles_down = UNIT_MESH_Y // PATCH_SIDE
    destination = target_unit[:, :, 0]
    columns = jnp.arange(devices_grid, dtype=jnp.int32)
    same = destination[:, :, None] == destination[:, None, :]
    lines = jnp.arange(blocks_here, dtype=jnp.int32)
    earlier = lines[None, :] < lines[:, None]
    position = jnp.sum((same & earlier[None]).astype(jnp.int32), axis=2)
    slot_index = destination * capacity + position
    slots = jnp.arange(devices_grid * capacity, dtype=jnp.int32)
    place = (slot_index[:, :, None] == slots).astype(jnp.float32)
    outgoing = jnp.einsum("kbs,kbc->ksc", place, parcel_patch, precision=high)
    labels = jnp.sum(place * (target_patch.astype(jnp.float32) + 1.0)[:, :, None], axis=1) - 1.0
    arrived, arrived_tile = (
        lax.all_to_all(
            outgoing.reshape(dies_here, devices_grid, capacity, cells_tile),
            ("row", "col"),
            split_axis=1,
            concat_axis=1,
            tiled=True,
        ),
        lax.all_to_all(
            labels.reshape(dies_here, devices_grid, capacity),
            ("row", "col"),
            split_axis=1,
            concat_axis=1,
            tiled=True,
        ),
    )
    incoming = arrived.reshape(dies_here, -1, cells_tile)
    target = arrived_tile.reshape(dies_here, -1).astype(jnp.int32)
    chosen = (target[:, :, None] == lines).astype(jnp.float32)
    patch_totals_acc = jnp.einsum("kst,ksc->ktc", chosen, incoming, precision=high)
    wattage_field = tiles_to_map(patch_totals_acc, tiles_down)
    first_die = lax.axis_index("die") * dies_here
    own_columns = lax.dynamic_slice_in_dim(source_heated_mixing, first_die, dies_here, 2)
    own_rows = lax.dynamic_slice_in_dim(source_heated_mixing, first_die, dies_here, 1)
    chip_heat_increase = stage(wattage_field, across_taps, down_taps, own_columns, False)
    adjoint_field_map = stage(
        chip_heat_increase, across_taps[:, ::-1], down_taps[:, ::-1], own_rows.transpose(0, 2, 1), True
    )
    adjoint_patches = map_to_tiles(adjoint_field_map, tiles_down)
    answers = jnp.einsum("kst,ktc->ksc", chosen, adjoint_patches, precision=high)
    returned = lax.all_to_all(
        answers.reshape(dies_here, devices_grid, capacity, cells_tile),
        ("row", "col"),
        split_axis=1,
        concat_axis=1,
        tiled=True,
    )
    block_power_slopes = jnp.einsum(
        "kbs,ksc->kbc", place, returned.reshape(dies_here, -1, cells_tile), precision=high
    )
    return (chip_heat_increase, block_power_slopes)


def solution(mesh):
    placed = (
        P("die", ("row", "col"), None),
        P("die", ("row", "col"), None),
        P("die", ("row", "col")),
        P(),
        P(),
        P(),
    )
    return jax.shard_map(
        local,
        mesh=mesh,
        in_specs=placed,
        out_specs=(P("die", "row", "col"), P("die", ("row", "col"), None)),
        check_vma=False,
    )
```

profile of v0, /device:TPU:0, one launch (start us, length us, event | category | flops | bytes accessed | tf_op | source)
XLA Modules:
  0.0 119.0 jit_solution(14679361998844307465)
XLA Ops:
  0.7 0.7 convert_add_fusion
  1.4 0.9 convert_reduce_fusion
  2.4 0.7 fusion.8
  3.3 0.6 copy.54
  3.9 7.4 %all-to-all-start = ((f32[2,16,16]{2,0,1:T(2,128)}), f32[2,16,16]{2,0,1:T(2,128)S(1)}, u32[]{:S(2)}, u32[]{:S(2)}) async-start(f32[2,16,16]{2,0,1:T(2,128)} %copy.54), calls=%async_computation | async-start | bytes 32768 | tf_op jit(solution)/shard_map/all_to_all | solution.py:245
  11.3 0.4 fusion.3
  11.7 0.8 copy.57
  12.5 5.2 %all-to-all-done = f32[2,16,16]{2,0,1:T(2,128)S(1)} async-done(((f32[2,16,16]{2,0,1:T(2,128)}), f32[2,16,16]{2,0,1:T(2,128)S(1)}, u32[]{:S(2)}, u32[]{:S(2)}) %all-to-all-start) | async-done | bytes 2080 | tf_op jit(solution)/shard_map/all_to_all | solution.py:245
  17.8 3.6 %all-to-all-start.1 = ((f32[2,16,16,256]{3,2,0,1:T(8,128)}), f32[2,16,16,256]{3,2,0,1:T(8,128)S(1)}, u32[]{:S(2)}, u32[]{:S(2)}) async-start(f32[2,16,16,256]{3,2,0,1:T(8,128)} %copy.57), calls=%async_computation.1 | async-start | bytes 1048576 | tf_op jit(solution)/shard_map/all_to_all | solution.py:238
  21.6 0.1 reverse.1
  22.4 13.4 %all-to-all-done.1 = f32[2,16,16,256]{3,2,0,1:T(8,128)S(1)} async-done(((f32[2,16,16,256]{3,2,0,1:T(8,128)}), f32[2,16,16,256]{3,2,0,1:T(8,128)S(1)}, u32[]{:S(2)}, u32[]{:S(2)}) %all-to-all-start.1) | async-done | bytes 524320 | tf_op jit(solution)/shard_map/all_to_all | solution.py:238
  35.8 0.4 fusion.1
  36.3 0.6 reshape.62
  36.9 2.0 %copy.71 = f32[2,8,16,16,16]{4,2,3,1,0:T(8,128)} copy(f32[2,8,16,16,16]{4,3,2,1,0:T(8,128)S(1)} %reshape.62) | data formatting | bytes 524288 | tf_op jit(solution)/shard_map/reshape | solution.py:205
  38.9 2.4 %reshape.63.x_ref = f32[2,128,256]{2,1,0:T(8,128)S(1)} reshape(f32[2,8,16,16,16]{4,3,2,1,0:T(8,128)} %bitcast.30) | data formatting | bytes 524288 | tf_op jit(solution)/shard_map/reshape | solution.py:208
  41.4 24.6 %shard_map.77.x_ref = f32[2,128,256]{2,1,0:T(8,128)S(1)} custom-call(f32[2,128,256]{2,1,0:T(8,128)S(1)} %reshape.63.x_ref, f32[8,384]{1,0:T(8,128)S(1)} %pad.13.across_ref, f32[8,384]{1,0:T(8,128)S(1)} %pad.14.down_ref, f32[8,8]{1,0:T(8,128)S(1)} %copy.61.mix_ref), custom_call_target="tpu_custom_call" | custom-call | tf_op jit(solution)/shard_map/pallas_call | solution.py:181
  66.0 25.6 %shard_map.78 = f32[2,128,256]{2,1,0:T(8,128)S(1)} custom-call(f32[2,128,256]{2,1,0:T(8,128)S(1)} %shard_map.77.x_ref, f32[8,384]{1,0:T(8,128)S(1)} %pad.15.across_ref, f32[8,384]{1,0:T(8,128)S(1)} %pad.16.down_ref, f32[8,8]{1,0:T(8,128)S(1)} %copy.63.mix_ref), custom_call_target="tpu_custom_call" | custom-call | tf_op jit(solution)/shard_map/pallas_call | solution.py:181
  91.6 0.6 reshape.66
  92.3 2.0 %copy.64 = f32[2,8,16,16,16]{4,3,2,1,0:T(8,128)} copy(f32[2,8,16,16,16]{4,2,3,1,0:T(8,128)S(1)} %bitcast.31) | data formatting | bytes 524288 | tf_op jit(solution)/shard_map/transpose | solution.py:218
  94.3 2.4 %reshape.67 = f32[2,128,256]{2,1,0:T(8,128)S(1)} reshape(f32[2,8,16,16,16]{4,3,2,1,0:T(8,128)} %copy.64) | data formatting | bytes 524288 | tf_op jit(solution)/shard_map/reshape | solution.py:218
  96.7 0.3 fusion
  97.1 20.1 %all_to_all.15 = f32[2,16,16,256]{3,2,0,1:T(8,128)S(1)} all-to-all(f32[2,16,16,256]{3,2,0,1:T(8,128)S(1)} %copy.65), channel_id=1, replica_groups=mesh['die'=2,'row'=4,'col'=4] {'row','col'}, dimensions={1} | all-to-all | bytes 1048576 | tf_op jit(solution)/shard_map/all_to_all | solution.py:267
  117.3 1.0 fusion.2
  118.3 0.7 copy.73
  (29 shorter events, 1.2 us)
Async XLA Ops:
  0.6 10.7 %copy-start = (f32[2,128,256]{2,1,0:T(8,128)S(1)}, f32[2,128,256]{2,1,0:T(8,128)}, u32[]{:S(2)}) copy-start(f32[2,128,256]{2,1,0:T(8,128)} %param.6) | copy-start | bytes 786436
  0.6 20.7 %copy-start.3 = (f32[8,4,4]{0,2,1:T(4,128)S(1)}, f32[8,4,4]{0,2,1:T(4,128)}, u32[]{:S(2)}) copy-start(f32[8,4,4]{0,2,1:T(4,128)} %param.11) | copy-start | bytes 1540
  0.7 20.9 %copy-start.1 = (f32[8,255]{1,0:T(8,128)S(1)}, f32[8,255]{1,0:T(8,128)}, u32[]{:S(2)}) copy-start(f32[8,255]{1,0:T(8,128)} %param.10) | copy-start | bytes 24484
  0.7 21.3 %copy-start.2 = (f32[8,255]{1,0:T(8,128)S(1)}, f32[8,255]{1,0:T(8,128)}, u32[]{:S(2)}) copy-start(f32[8,255]{1,0:T(8,128)} %param.9) | copy-start | bytes 24484
  3.9 13.9 %all-to-all-start = ((f32[2,16,16]{2,0,1:T(2,128)}), f32[2,16,16]{2,0,1:T(2,128)S(1)}, u32[]{:S(2)}, u32[]{:S(2)}) async-start(f32[2,16,16]{2,0,1:T(2,128)} %copy.54), calls=%async_computation | async-start | bytes 32768 | tf_op jit(solution)/shard_map/all_to_all | solution.py:245
  17.8 18.0 %all-to-all-start.1 = ((f32[2,16,16,256]{3,2,0,1:T(8,128)}), f32[2,16,16,256]{3,2,0,1:T(8,128)S(1)}, u32[]{:S(2)}, u32[]{:S(2)}) async-start(f32[2,16,16,256]{3,2,0,1:T(8,128)} %copy.57), calls=%async_computation.1 | async-start | bytes 1048576 | tf_op jit(solution)/shard_map/all_to_all | solution.py:238
where the time goes:
time: 119 us
  Pallas kernels  50.2 us (42%)
  blocking collectives  20.1 us (17%)
  waiting for transfers between devices  18.6 us (16%)
  local copies, waits for them, and re-layouts  13.5 us (11%)
  starting transfers between devices  10.9 us (9%)
  other arithmetic  2.53 us (2%)
  matrix products  2.19 us (2%)
    pallas_call x2, Pallas kernels, stage(): pl.pallas_call(functools.partial(stage_kernel, is_seed), out_shape=jax.Sh...  50.2 us
    all_to_all x1, blocking collectives, local(): lax.all_to_all(answers.reshape(dies_here, devices_grid, capacity, cells_t...  20.1 us
    all_to_all x1, waiting for transfers between devices, local(): lax.all_to_all(outgoing.reshape(dies_here, devices_grid, capacity, cells_...  13.4 us
    all_to_all x1, starting transfers between devices, local(): lax.all_to_all(labels.reshape(dies_here, devices_grid, capacity), ('row',...  7.36 us
    all_to_all x1, waiting for transfers between devices, local(): lax.all_to_all(labels.reshape(dies_here, devices_grid, capacity), ('row',...  5.24 us
    all_to_all x1, starting transfers between devices, local(): lax.all_to_all(outgoing.reshape(dies_here, devices_grid, capacity, cells_...  3.57 us
    reshape x2, local copies, waits for them, and re-layouts, tiles_to_map(): patch_totals_acc.reshape(dies_here, tile_total // tiles_down, tiles_down,...  2.64 us
    reshape x1, local copies, waits for them, and re-layouts, tiles_to_map(): mesh_layout.transpose(0, 1, 3, 2, 4)  2.44 us
  transfers between devices with their start and end apart: 2, of which 2 were waited for; matrix products, arithmetic and copies ran while one was open for 2% of the time, Pallas kernels for 0%

commit v1 on v0

--- a/solution.py
+++ b/solution.py
@@ -200,6 +200,78 @@
     )(fields, bases(across_taps), bases(down_taps), mix.reshape(terms, dies * here))
 
 
+def swap_kernel(*refs):
+    count = (len(refs) - 3) // 2
+    sources, landed = refs[:count], refs[count : 2 * count]
+    send, recv, keep = refs[2 * count :]
+    across = lax.axis_size("col")
+    peers = across * lax.axis_size("row")
+    me = lax.axis_index("row") * across + lax.axis_index("col")
+    barrier = pltpu.get_barrier_semaphore()
+
+    def place(number):
+        return {"row": number // across, "col": number % across}
+
+    def greet(i, carry):
+        pl.semaphore_signal(
+            barrier, inc=1, device_id=place((me + i) % peers), device_id_type=pl.DeviceIdType.MESH
+        )
+        return carry
+
+    def copies(i):
+        to = (me + i) % peers
+        return [
+            pltpu.make_async_remote_copy(
+                src_ref=src.at[:, to], dst_ref=dst.at[:, me],
+                send_sem=send.at[k, i], recv_sem=recv.at[k, i],
+                device_id=place(to), device_id_type=pl.DeviceIdType.MESH,
+            )
+            for k, (src, dst) in enumerate(zip(sources, landed))
+        ]
+
+    def begin(i, carry):
+        for c in copies(i):
+            c.start()
+        return carry
+
+    def finish(i, carry):
+        for c in copies(i):
+            c.wait()
+        return carry
+
+    lax.fori_loop(1, peers, greet, 0)
+    pl.semaphore_wait(barrier, peers - 1)
+    lax.fori_loop(1, peers, begin, 0)
+    stay = [
+        pltpu.make_async_copy(src.at[:, me], dst.at[:, me], keep.at[k])
+        for k, (src, dst) in enumerate(zip(sources, landed))
+    ]
+    for c in stay:
+        c.start()
+    for c in stay:
+        c.wait()
+    lax.fori_loop(1, peers, finish, 0)
+
+
+def swap(arrays, number):
+    count, peers = len(arrays), arrays[0].shape[1]
+    vmem = pl.BlockSpec(memory_space=pltpu.VMEM)
+    return pl.pallas_call(
+        swap_kernel,
+        out_shape=[jax.ShapeDtypeStruct(x.shape, x.dtype) for x in arrays],
+        in_specs=[vmem] * count,
+        out_specs=[vmem] * count,
+        scratch_shapes=[
+            pltpu.SemaphoreType.DMA((count, peers)),
+            pltpu.SemaphoreType.DMA((count, peers)),
+            pltpu.SemaphoreType.DMA((count,)),
+        ],
+        compiler_params=pltpu.CompilerParams(
+            collective_id=number, has_side_effects=True, vmem_limit_bytes=24 * 2**20
+        ),
+    )(*arrays)
+
+
 def tiles_to_map(patch_totals_acc, tiles_down):
     dies_here, tile_total, cell_count = patch_totals_acc.shape
     mesh_layout = patch_totals_acc.reshape(
@@ -234,23 +306,14 @@
     place = (slot_index[:, :, None] == slots).astype(jnp.float32)
     outgoing = jnp.einsum("kbs,kbc->ksc", place, parcel_patch, precision=high)
     labels = jnp.sum(place * (target_patch.astype(jnp.float32) + 1.0)[:, :, None], axis=1) - 1.0
-    arrived, arrived_tile = (
-        lax.all_to_all(
-            outgoing.reshape(dies_here, devices_grid, capacity, cells_tile),
-            ("row", "col"),
-            split_axis=1,
-            concat_axis=1,
-            tiled=True,
-        ),
-        lax.all_to_all(
-            labels.reshape(dies_here, devices_grid, capacity),
-            ("row", "col"),
-            split_axis=1,
-            concat_axis=1,
-            tiled=True,
-        ),
+    span = dies_here * capacity
+    rows = labels.reshape(dies_here, devices_grid, capacity).transpose(1, 0, 2).reshape(1, devices_grid, 1, span)
+    rows = jnp.pad(rows, ((0, 0), (0, 0), (0, 0), (0, 128 - span)))
+    arrived, arrived_rows = swap(
+        (outgoing.reshape(dies_here, devices_grid, capacity, cells_tile), rows), 2
     )
     incoming = arrived.reshape(dies_here, -1, cells_tile)
+    arrived_tile = arrived_rows[0, :, 0, :span].reshape(devices_grid, dies_here, capacity).transpose(1, 0, 2)
     target = arrived_tile.reshape(dies_here, -1).astype(jnp.int32)
     chosen = (target[:, :, None] == lines).astype(jnp.float32)
     patch_totals_acc = jnp.einsum("kst,ksc->ktc", chosen, incoming, precision=high)
@@ -264,13 +327,7 @@
     )
     adjoint_patches = map_to_tiles(adjoint_field_map, tiles_down)
     answers = jnp.einsum("kst,ktc->ksc", chosen, adjoint_patches, precision=high)
-    returned = lax.all_to_all(
-        answers.reshape(dies_here, devices_grid, capacity, cells_tile),
-        ("row", "col"),
-        split_axis=1,
-        concat_axis=1,
-        tiled=True,
-    )
+    (returned,) = swap((answers.reshape(dies_here, devices_grid, capacity, cells_tile),), 3)
     block_power_slopes = jnp.einsum(
         "kbs,ksc->kbc", place, returned.reshape(dies_here, -1, cells_tile), precision=high
     )

time: 119 us -> 109 us (0.916)
  the two profiles are of different devices: /device:TPU:0 before, /device:TPU:11 now
where the time goes in v1:
time: 109 us; the launch traced here: 108 us
  Pallas kernels  86.3 us (79%)
  local copies, waits for them, and re-layouts  16.3 us (15%)
  other arithmetic  2.54 us (2%)
  matrix products  2.2 us (2%)
    pallas_call x2, Pallas kernels, stage(): pl.pallas_call(functools.partial(stage_kernel, is_seed), out_shape=jax.Sh...  49 us
    pallas_call x2, Pallas kernels, swap(): pl.pallas_call(swap_kernel, out_shape=[jax.ShapeDtypeStruct(x.shape, x.dt...  37.3 us
    reshape x2, local copies, waits for them, and re-layouts, tiles_to_map(): patch_totals_acc.reshape(dies_here, tile_total // tiles_down, tiles_down,...  2.66 us
    unnamed x7, local copies, waits for them, and re-layouts  2.52 us
    reshape x1, local copies, waits for them, and re-layouts, map_to_tiles(): mesh_layout.transpose(0, 1, 3, 2, 4)  2.44 us
    reshape x1, local copies, waits for them, and re-layouts, tiles_to_map(): mesh_layout.transpose(0, 1, 3, 2, 4)  2.44 us

profile of v1, /device:TPU:11, one launch (start us, length us, event | category | flops | bytes accessed | tf_op | source)
XLA Modules:
  0.0 108.1 jit_solution(15308045540908817582)
XLA Ops:
  0.6 0.7 convert_add_fusion
  1.4 0.7 dynamic-slice_bitcast_fusion
  2.1 0.7 constant_dynamic-slice_fusion
  2.9 0.8 reverse.1
  3.9 0.8 reverse
  4.9 0.8 pad.18.across_ref
  5.7 0.8 pad.19.down_ref
  6.4 0.9 convert_reduce_fusion
  7.4 0.7 fusion.8
  8.4 0.4 fusion.3
  8.8 17.4 %shard_map.77 = (f32[2,16,16,256]{3,2,1,0:T(8,128)S(1)}, f32[1,16,1,128]{3,2,1,0:T(1,128)S(1)}) custom-call(f32[2,16,16,256]{3,2,1,0:T(8,128)S(1)} %bitcast.34, f32[1,16,1,128]{3,2,1,0:T(1,128)S(1)} %pad.17.refs_1_), custom_call_target="tpu_custom_call" | custom-call | tf_op jit(solution)/shard_map/pallas_call | solution.py:259
  26.5 0.5 fusion.1
  26.9 0.6 reshape.67
  27.6 2.0 %copy.38 = f32[2,8,16,16,16]{4,2,3,1,0:T(8,128)} copy(f32[2,8,16,16,16]{4,3,2,1,0:T(8,128)S(1)} %reshape.67) | data formatting | bytes 524288 | tf_op jit(solution)/shard_map/reshape | solution.py:277
  29.6 2.4 %reshape.68.x_ref = f32[2,128,256]{2,1,0:T(8,128)S(1)} reshape(f32[2,8,16,16,16]{4,3,2,1,0:T(8,128)} %bitcast.38) | data formatting | bytes 524288 | tf_op jit(solution)/shard_map/reshape | solution.py:280
  32.0 24.5 %shard_map.78.x_ref = f32[2,128,256]{2,1,0:T(8,128)S(1)} custom-call(f32[2,128,256]{2,1,0:T(8,128)S(1)} %reshape.68.x_ref, f32[8,384]{1,0:T(8,128)S(1)} %pad.18.across_ref, f32[8,384]{1,0:T(8,128)S(1)} %pad.19.down_ref, f32[8,8]{1,0:T(8,128)S(1)} %copy.30.mix_ref), custom_call_target="tpu_custom_call" | custom-call | tf_op jit(solution)/shard_map/pallas_call | solution.py:181
  56.6 24.4 %shard_map.79 = f32[2,128,256]{2,1,0:T(8,128)S(1)} custom-call(f32[2,128,256]{2,1,0:T(8,128)S(1)} %shard_map.78.x_ref, f32[8,384]{1,0:T(8,128)S(1)} %pad.20.across_ref, f32[8,384]{1,0:T(8,128)S(1)} %pad.21.down_ref, f32[8,8]{1,0:T(8,128)S(1)} %copy.32.mix_ref), custom_call_target="tpu_custom_call" | custom-call | tf_op jit(solution)/shard_map/pallas_call | solution.py:181
  81.0 0.6 reshape.71
  81.7 2.0 %copy.33 = f32[2,8,16,16,16]{4,3,2,1,0:T(8,128)} copy(f32[2,8,16,16,16]{4,2,3,1,0:T(8,128)S(1)} %bitcast.39) | data formatting | bytes 524288 | tf_op jit(solution)/shard_map/transpose | solution.py:290
  83.7 2.4 %reshape.72 = f32[2,128,256]{2,1,0:T(8,128)S(1)} reshape(f32[2,8,16,16,16]{4,3,2,1,0:T(8,128)} %copy.33) | data formatting | bytes 524288 | tf_op jit(solution)/shard_map/reshape | solution.py:290
  86.1 0.4 fusion
  86.5 19.9 %shard_map.80 = f32[2,16,16,256]{3,2,1,0:T(8,128)S(1)} custom-call(f32[2,16,16,256]{3,2,1,0:T(8,128)S(1)} %bitcast.35), custom_call_target="tpu_custom_call" | custom-call | tf_op jit(solution)/shard_map/pallas_call | solution.py:259
  106.4 1.0 fusion.2
  107.4 0.7 copy.41
  (20 shorter events, 1.0 us)
Async XLA Ops:
  0.6 7.8 %copy-start = (f32[2,128,256]{2,1,0:T(8,128)S(1)}, f32[2,128,256]{2,1,0:T(8,128)}, u32[]{:S(2)}) copy-start(f32[2,128,256]{2,1,0:T(8,128)} %param.6) | copy-start | bytes 786436

commit v2 on v1

--- a/solution.py
+++ b/solution.py
@@ -88,7 +88,7 @@
     start(has_right, to_right[1])
 
     def across_bands(t):
-        span = jnp.broadcast_to(across_ref[pl.ds(t, 1), :], (a, a + 2 * h))
+        span = jnp.broadcast_to(across_base[t : t + 1, :], (a, a + 2 * h))
         head, rest = two_halves(pltpu.roll(span, 0, 1, stride=1, stride_axis=0))
         lines = pl.ds(t * a, a)
         w = a + 2 * h
@@ -98,7 +98,7 @@
 
     def down_bands(t):
         w = b + 2 * h
-        span = jnp.broadcast_to(down_ref[pl.ds(t, 1), :], (h, 3 * h))
+        span = jnp.broadcast_to(down_base[t : t + 1, :], (h, 3 * h))
         head, rest = two_halves(pltpu.roll(span, 0, 1, stride=1, stride_axis=0))
         for part in range(3):
             piece = rest if part == 1 else head
@@ -111,6 +111,16 @@
                 if hi < w:
                     d_cat[t, lines, part * w + hi : part * w + w] = jnp.zeros((h, w - hi), jnp.bfloat16)
 
+    def base(taps_ref):
+        taps = taps_ref.shape[1]
+        k = lax.broadcasted_iota(jnp.int32, (taps, 3 * h), 0)
+        u = lax.broadcasted_iota(jnp.int32, (taps, 3 * h), 1)
+        pick = (u == (taps - k if is_seed else k + 1)).astype(jnp.float32)
+        return jnp.dot(
+            taps_ref[...], pick, precision=lax.Precision.HIGHEST, preferred_element_type=jnp.float32
+        )
+
+    across_base, down_base = base(across_ref), base(down_ref)
     for t in range(terms):
         across_bands(t)
     arrived(has_down, to_up)
@@ -119,32 +129,54 @@
     arrived(has_up, to_down)
     for c, there in ((to_left[0], has_left), (to_right[0], has_right)):
         start(jnp.logical_and(has_up, there), c)
+    w0, w1 = a + 2 * h, b + 2 * h
+
+    def fill(e, source, at, width):
+        head, rest = two_halves(pad[e, :, source : source + width])
+        cols = slice(e * w1 + at, e * w1 + at + width)
+        p_cat[0:w0, cols] = head
+        p_cat[w0 : 2 * w0, cols] = rest
+        p_cat[2 * w0 : 3 * w0, cols] = head
+
+    def across(at, width):
+        cols = slice(at, at + width)
+        y_all[:, cols] = jnp.dot(a_cat[...], p_cat[:, cols], preferred_element_type=jnp.float32)
+
+    for e in range(here):
+        fill(e, h, 0, b)
+        across(e * w1, b)
     for t in range(terms):
         down_bands(t)
     rows_of = (has_up, None, has_down)
     for k in range(3):
         for there, c in ((has_right, to_left[k]), (has_left, to_right[k])):
             arrived(there if k == 1 else jnp.logical_and(rows_of[k], there), c)
-
-    w0, w1 = a + 2 * h, b + 2 * h
     for e in range(here):
-        head, rest = two_halves(pad[e])
-        cols = pl.ds(e * w1, w1)
-        p_cat[0:w0, cols] = head
-        p_cat[w0 : 2 * w0, cols] = rest
-        p_cat[2 * w0 : 3 * w0, cols] = head
-
-    def across(n, carry):
-        cols = pl.ds(pl.multiple_of(n * 256, 256), 256)
-        y_all[:, cols] = jnp.dot(a_cat[...], p_cat[:, cols], preferred_element_type=jnp.float32)
-        return carry
-
-    lax.fori_loop(0, here * w1 // 256, across, 0)
+        fill(e, 0, b, h)
+        fill(e, h + b, b + h, h)
+        across(e * w1 + b, 2 * h)
     acc[...] = jnp.zeros_like(acc)
+
+    def weight(t, d, e):
+        mine = die * here + e
+        return mix_ref[t, mine * acc.shape[0] + d if is_seed else d * acc.shape[0] + mine]
 
     def along(t, carry):
         lines = pl.ds(pl.multiple_of(t * a, a), a)
-        rows = jnp.concatenate([y_all[lines, e * w1 : (e + 1) * w1] for e in range(here)], axis=0)
+        rows = jnp.concatenate(
+            [
+                jnp.concatenate(
+                    [
+                        y_all[lines, e * w1 + b : e * w1 + b + h],
+                        y_all[lines, e * w1 : e * w1 + b],
+                        y_all[lines, e * w1 + b + h : (e + 1) * w1],
+                    ],
+                    axis=1,
+                )
+                for e in range(here)
+            ],
+            axis=0,
+        )
         head, rest = two_halves(rows)
         z = lax.dot_general(
             jnp.concatenate([head, head, rest], axis=1), d_cat[t],
@@ -153,7 +185,7 @@
         for d in range(acc.shape[0]):
             total = acc[d]
             for e in range(here):
-                total = total + mix_ref[t, d * here + e] * z[e * a : (e + 1) * a]
+                total = total + weight(t, d, e) * z[e * a : (e + 1) * a]
             acc[d] = total
         return carry
 
@@ -167,10 +199,6 @@
             ended(jnp.logical_and(rows_of[k], there), c)
     share.wait()
     out_ref[...] = acc[pl.ds(die * here, here)] + got[...]
-
-
-def bases(taps):
-    return jnp.pad(taps, ((0, 0), (1, 3 * HALO - 1 - taps.shape[1])))
 
 
 def stage(fields, across_taps, down_taps, mix, is_seed):
@@ -197,7 +225,7 @@
         compiler_params=pltpu.CompilerParams(
             collective_id=1 if is_seed else 0, has_side_effects=True, vmem_limit_bytes=48 * 2**20
         ),
-    )(fields, bases(across_taps), bases(down_taps), mix.reshape(terms, dies * here))
+    )(fields, across_taps, down_taps, mix.reshape(terms, dies * dies))
 
 
 def swap_kernel(*refs):
@@ -230,7 +258,7 @@
         ]
 
     def begin(i, carry):
-        for c in copies(i):
+        for c in copies((i + peers // 2 - 2) % (peers - 1) + 1):
             c.start()
         return carry
 
@@ -318,13 +346,8 @@
     chosen = (target[:, :, None] == lines).astype(jnp.float32)
     patch_totals_acc = jnp.einsum("kst,ksc->ktc", chosen, incoming, precision=high)
     wattage_field = tiles_to_map(patch_totals_acc, tiles_down)
-    first_die = lax.axis_index("die") * dies_here
-    own_columns = lax.dynamic_slice_in_dim(source_heated_mixing, first_die, dies_here, 2)
-    own_rows = lax.dynamic_slice_in_dim(source_heated_mixing, first_die, dies_here, 1)
-    chip_heat_increase = stage(wattage_field, across_taps, down_taps, own_columns, False)
-    adjoint_field_map = stage(
-        chip_heat_increase, across_taps[:, ::-1], down_taps[:, ::-1], own_rows.transpose(0, 2, 1), True
-    )
+    chip_heat_increase = stage(wattage_field, across_taps, down_taps, source_heated_mixing, False)
+    adjoint_field_map = stage(chip_heat_increase, across_taps, down_taps, source_heated_mixing, True)
     adjoint_patches = map_to_tiles(adjoint_field_map, tiles_down)
     answers = jnp.einsum("kst,ktc->ksc", chosen, adjoint_patches, precision=high)
     (returned,) = swap((answers.reshape(dies_here, devices_grid, capacity, cells_tile),), 3)

time: 109 us -> 102 us (0.936)
  the two profiles are of different devices: /device:TPU:11 before, /device:TPU:0 now
where the time goes in v2:
time: 102 us
  Pallas kernels  84.6 us (83%)
  local copies, waits for them, and re-layouts  12.1 us (12%)
  other arithmetic  2.54 us (2%)
  matrix products  2.21 us (2%)
    pallas_call x2, Pallas kernels, stage(): pl.pallas_call(functools.partial(stage_kernel, is_seed), out_shape=jax.Sh...  47.4 us
    pallas_call x2, Pallas kernels, swap(): pl.pallas_call(swap_kernel, out_shape=[jax.ShapeDtypeStruct(x.shape, x.dt...  37.1 us
    reshape x2, local copies, waits for them, and re-layouts, tiles_to_map(): patch_totals_acc.reshape(dies_here, tile_total // tiles_down, tiles_down,...  2.66 us
    reshape x1, local copies, waits for them, and re-layouts, tiles_to_map(): mesh_layout.transpose(0, 1, 3, 2, 4)  2.47 us
    reshape x1, local copies, waits for them, and re-layouts, map_to_tiles(): mesh_layout.transpose(0, 1, 3, 2, 4)  2.44 us

profile of v2, /device:TPU:0, one launch (start us, length us, event | category | flops | bytes accessed | tf_op | source)
XLA Modules:
  0.0 102.2 jit_solution(5120981366917262836)
XLA Ops:
  0.6 0.7 convert_add_fusion
  1.4 0.8 copy.28.mix_ref
  2.2 0.9 convert_reduce_fusion
  3.1 0.7 fusion.8
  3.8 0.1 select_reduce_fusion
  3.9 0.1 sub.7
  4.0 0.1 reshape.63
  4.1 0.4 fusion.3
  4.6 19.8 %shard_map.77 = (f32[2,16,16,256]{3,2,1,0:T(8,128)S(1)}, f32[1,16,1,128]{3,2,1,0:T(1,128)S(1)}) custom-call(f32[2,16,16,256]{3,2,1,0:T(8,128)S(1)} %bitcast.29, f32[1,16,1,128]{3,2,1,0:T(1,128)S(1)} %pad.4.refs_1_), custom_call_target="tpu_custom_call" | custom-call | tf_op jit(solution)/shard_map/pallas_call | solution.py:287
  24.4 0.1 convert_element_type.29
  24.5 0.1 convert_element_type.31
  24.5 0.5 fusion.1
  25.0 0.6 reshape.65
  25.7 2.0 %copy.35 = f32[2,8,16,16,16]{4,2,3,1,0:T(8,128)} copy(f32[2,8,16,16,16]{4,3,2,1,0:T(8,128)S(1)} %reshape.65) | data formatting | bytes 524288 | tf_op jit(solution)/shard_map/reshape | solution.py:305
  27.7 2.5 %reshape.66.x_ref = f32[2,128,256]{2,1,0:T(8,128)S(1)} reshape(f32[2,8,16,16,16]{4,3,2,1,0:T(8,128)} %bitcast.33) | data formatting | bytes 524288 | tf_op jit(solution)/shard_map/reshape | solution.py:308
  30.2 23.3 %shard_map.78.x_ref = f32[2,128,256]{2,1,0:T(8,128)S(1)} custom-call(f32[2,128,256]{2,1,0:T(8,128)S(1)} %reshape.66.x_ref, f32[8,255]{1,0:T(8,128)S(1)} %copy-done.1, f32[8,255]{1,0:T(8,128)S(1)} %copy-done.2, f32[8,16]{1,0:T(8,128)S(1)} %copy.28.mix_ref), custom_call_target="tpu_custom_call" | custom-call | tf_op jit(solution)/shard_map/pallas_call | solution.py:209
  53.5 24.2 %shard_map.79 = f32[2,128,256]{2,1,0:T(8,128)S(1)} custom-call(f32[2,128,256]{2,1,0:T(8,128)S(1)} %shard_map.78.x_ref, f32[8,255]{1,0:T(8,128)S(1)} %copy-done.1, f32[8,255]{1,0:T(8,128)S(1)} %copy-done.2, f32[8,16]{1,0:T(8,128)S(1)} %copy.28.mix_ref), custom_call_target="tpu_custom_call" | custom-call | tf_op jit(solution)/shard_map/pallas_call | solution.py:209
  77.6 0.6 reshape.68
  78.3 2.0 %copy.30 = f32[2,8,16,16,16]{4,3,2,1,0:T(8,128)} copy(f32[2,8,16,16,16]{4,2,3,1,0:T(8,128)S(1)} %bitcast.34) | data formatting | bytes 524288 | tf_op jit(solution)/shard_map/transpose | solution.py:318
  80.3 2.4 %reshape.69 = f32[2,128,256]{2,1,0:T(8,128)S(1)} reshape(f32[2,8,16,16,16]{4,3,2,1,0:T(8,128)} %copy.30) | data formatting | bytes 524288 | tf_op jit(solution)/shard_map/reshape | solution.py:318
  82.8 0.4 fusion
  83.1 17.4 %shard_map.80 = f32[2,16,16,256]{3,2,1,0:T(8,128)S(1)} custom-call(f32[2,16,16,256]{3,2,1,0:T(8,128)S(1)} %bitcast.30), custom_call_target="tpu_custom_call" | custom-call | tf_op jit(solution)/shard_map/pallas_call | solution.py:287
  100.5 1.0 fusion.2
  101.5 0.7 copy.38
  (12 shorter events, 0.1 us)
Async XLA Ops:
  0.6 3.5 %copy-start = (f32[2,128,256]{2,1,0:T(8,128)S(1)}, f32[2,128,256]{2,1,0:T(8,128)}, u32[]{:S(2)}) copy-start(f32[2,128,256]{2,1,0:T(8,128)} %param.6) | copy-start | bytes 786436
  27.7 2.5 %copy-start.1 = (f32[8,255]{1,0:T(8,128)S(1)}, f32[8,255]{1,0:T(8,128)}, u32[]{:S(2)}) copy-start(f32[8,255]{1,0:T(8,128)} %across_ref.3) | copy-start | bytes 24484
  27.7 2.5 %copy-start.2 = (f32[8,255]{1,0:T(8,128)S(1)}, f32[8,255]{1,0:T(8,128)}, u32[]{:S(2)}) copy-start(f32[8,255]{1,0:T(8,128)} %down_ref.3) | copy-start | bytes 24484

commit v3 on v2

--- a/solution.py
+++ b/solution.py
@@ -161,8 +161,11 @@
         mine = die * here + e
         return mix_ref[t, mine * acc.shape[0] + d if is_seed else d * acc.shape[0] + mine]
 
-    def along(t, carry):
-        lines = pl.ds(pl.multiple_of(t * a, a), a)
+    part = a // 2
+
+    def along(half, t, carry):
+        lines = pl.ds(pl.multiple_of(t * a + half * part, part), part)
+        some = slice(half * part, (half + 1) * part)
         rows = jnp.concatenate(
             [
                 jnp.concatenate(
@@ -183,21 +186,26 @@
             (((1,), (1,)), ((), ())), preferred_element_type=jnp.float32,
         )
         for d in range(acc.shape[0]):
-            total = acc[d]
+            total = acc[d, some]
             for e in range(here):
-                total = total + weight(t, d, e) * z[e * a : (e + 1) * a]
-            acc[d] = total
+                total = total + weight(t, d, e) * z[e * part : (e + 1) * part]
+            acc[d, some] = total
         return carry
 
-    lax.fori_loop(0, terms, along, 0)
-    share = copy(8, acc.at[pl.ds((1 - die) * here, here)], got, other)
-    share.start()
+    shares = []
+    for half in range(2):
+        lax.fori_loop(0, terms, functools.partial(along, half), 0)
+        some = pl.ds(half * part, part)
+        share = copy(8 + half, acc.at[pl.ds((1 - die) * here, here), some], got.at[:, some], other)
+        share.start()
+        shares.append(share)
     for there, c in ((has_up, to_up), (has_down, to_down), (has_left, to_left[1]), (has_right, to_right[1])):
         ended(there, c)
     for k in (0, 2):
         for there, c in ((has_left, to_left[k]), (has_right, to_right[k])):
             ended(jnp.logical_and(rows_of[k], there), c)
-    share.wait()
+    for share in shares:
+        share.wait()
     out_ref[...] = acc[pl.ds(die * here, here)] + got[...]
 
 
@@ -219,8 +227,8 @@
             pltpu.VMEM((terms * a, here * w1), jnp.float32),
             pltpu.VMEM((dies, a, b), jnp.float32),
             pltpu.VMEM((here, a, b), jnp.float32),
-            pltpu.SemaphoreType.DMA((9,)),
-            pltpu.SemaphoreType.DMA((9,)),
+            pltpu.SemaphoreType.DMA((10,)),
+            pltpu.SemaphoreType.DMA((10,)),
         ],
         compiler_params=pltpu.CompilerParams(
             collective_id=1 if is_seed else 0, has_side_effects=True, vmem_limit_bytes=48 * 2**20

time: 102 us -> 105 us (1.029)
  Pallas kernels: 84.6 us -> 86.7 us
    pallas_call x2, Pallas kernels: 47.4 us -> 50.1 us  [stage(): pl.pallas_call(functools.partial(stage_kernel, is_seed), out_shape=jax.Sh...]
where the time goes in v3:
time: 105 us; the launch traced here: 104 us
  Pallas kernels  86.7 us (83%)
  local copies, waits for them, and re-layouts  12.1 us (12%)
  other arithmetic  2.54 us (2%)
  matrix products  2.2 us (2%)
    pallas_call x2, Pallas kernels, stage(): pl.pallas_call(functools.partial(stage_kernel, is_seed), out_shape=jax.Sh...  50.1 us
    pallas_call x2, Pallas kernels, swap(): pl.pallas_call(swap_kernel, out_shape=[jax.ShapeDtypeStruct(x.shape, x.dt...  36.6 us
    reshape x2, local copies, waits for them, and re-layouts, tiles_to_map(): patch_totals_acc.reshape(dies_here, tile_total // tiles_down, tiles_down,...  2.66 us
    reshape x1, local copies, waits for them, and re-layouts, tiles_to_map(): mesh_layout.transpose(0, 1, 3, 2, 4)  2.47 us
    reshape x1, local copies, waits for them, and re-layouts, map_to_tiles(): mesh_layout.transpose(0, 1, 3, 2, 4)  2.44 us

profile of v3, /device:TPU:0, one launch (start us, length us, event | category | flops | bytes accessed | tf_op | source)
XLA Modules:
  0.0 104.3 jit_solution(867944448979713076)
XLA Ops:
  0.6 0.7 convert_add_fusion
  1.4 0.8 copy.28.mix_ref
  2.2 0.9 convert_reduce_fusion
  3.1 0.7 fusion.8
  3.8 0.1 select_reduce_fusion
  3.9 0.1 sub.7
  4.0 0.1 reshape.63
  4.1 0.4 fusion.3
  4.6 19.8 %shard_map.77 = (f32[2,16,16,256]{3,2,1,0:T(8,128)S(1)}, f32[1,16,1,128]{3,2,1,0:T(1,128)S(1)}) custom-call(f32[2,16,16,256]{3,2,1,0:T(8,128)S(1)} %bitcast.29, f32[1,16,1,128]{3,2,1,0:T(1,128)S(1)} %pad.4.refs_1_), custom_call_target="tpu_custom_call" | custom-call | tf_op jit(solution)/shard_map/pallas_call | solution.py:295
  24.4 0.1 convert_element_type.29
  24.5 0.1 convert_element_type.31
  24.5 0.5 fusion.1
  25.0 0.6 reshape.65
  25.7 2.0 %copy.35 = f32[2,8,16,16,16]{4,2,3,1,0:T(8,128)} copy(f32[2,8,16,16,16]{4,3,2,1,0:T(8,128)S(1)} %reshape.65) | data formatting | bytes 524288 | tf_op jit(solution)/shard_map/reshape | solution.py:313
  27.7 2.5 %reshape.66.x_ref = f32[2,128,256]{2,1,0:T(8,128)S(1)} reshape(f32[2,8,16,16,16]{4,3,2,1,0:T(8,128)} %bitcast.33) | data formatting | bytes 524288 | tf_op jit(solution)/shard_map/reshape | solution.py:316
  30.2 23.6 %shard_map.78.x_ref = f32[2,128,256]{2,1,0:T(8,128)S(1)} custom-call(f32[2,128,256]{2,1,0:T(8,128)S(1)} %reshape.66.x_ref, f32[8,255]{1,0:T(8,128)S(1)} %copy-done.1, f32[8,255]{1,0:T(8,128)S(1)} %copy-done.2, f32[8,16]{1,0:T(8,128)S(1)} %copy.28.mix_ref), custom_call_target="tpu_custom_call" | custom-call | tf_op jit(solution)/shard_map/pallas_call | solution.py:217
  53.8 26.5 %shard_map.79 = f32[2,128,256]{2,1,0:T(8,128)S(1)} custom-call(f32[2,128,256]{2,1,0:T(8,128)S(1)} %shard_map.78.x_ref, f32[8,255]{1,0:T(8,128)S(1)} %copy-done.1, f32[8,255]{1,0:T(8,128)S(1)} %copy-done.2, f32[8,16]{1,0:T(8,128)S(1)} %copy.28.mix_ref), custom_call_target="tpu_custom_call" | custom-call | tf_op jit(solution)/shard_map/pallas_call | solution.py:217
  80.3 0.6 reshape.68
  81.0 2.0 %copy.30 = f32[2,8,16,16,16]{4,3,2,1,0:T(8,128)} copy(f32[2,8,16,16,16]{4,2,3,1,0:T(8,128)S(1)} %bitcast.34) | data formatting | bytes 524288 | tf_op jit(solution)/shard_map/transpose | solution.py:326
  83.0 2.4 %reshape.69 = f32[2,128,256]{2,1,0:T(8,128)S(1)} reshape(f32[2,8,16,16,16]{4,3,2,1,0:T(8,128)} %copy.30) | data formatting | bytes 524288 | tf_op jit(solution)/shard_map/reshape | solution.py:326
  85.4 0.4 fusion
  85.8 16.8 %shard_map.80 = f32[2,16,16,256]{3,2,1,0:T(8,128)S(1)} custom-call(f32[2,16,16,256]{3,2,1,0:T(8,128)S(1)} %bitcast.30), custom_call_target="tpu_custom_call" | custom-call | tf_op jit(solution)/shard_map/pallas_call | solution.py:295
  102.6 1.0 fusion.2
  103.6 0.7 copy.38
  (12 shorter events, 0.1 us)
Async XLA Ops:
  0.6 3.5 %copy-start = (f32[2,128,256]{2,1,0:T(8,128)S(1)}, f32[2,128,256]{2,1,0:T(8,128)}, u32[]{:S(2)}) copy-start(f32[2,128,256]{2,1,0:T(8,128)} %param.6) | copy-start | bytes 786436
  27.7 2.5 %copy-start.1 = (f32[8,255]{1,0:T(8,128)S(1)}, f32[8,255]{1,0:T(8,128)}, u32[]{:S(2)}) copy-start(f32[8,255]{1,0:T(8,128)} %across_ref.3) | copy-start | bytes 24484
  27.7 2.5 %copy-start.2 = (f32[8,255]{1,0:T(8,128)S(1)}, f32[8,255]{1,0:T(8,128)}, u32[]{:S(2)}) copy-start(f32[8,255]{1,0:T(8,128)} %down_ref.3) | copy-start | bytes 24484
